TPU v7x, 32 devices: a whole 2x2x4 slice. The times are simulated.
32 devices in a mesh: dp: 2 (over x), seq: 8 (over z, y), mp: 2 (over core).
Axes of the slice: x: 2, y: 2, z: 4, core: 2. Of those that a mesh axis runs over, the one named last changes fastest.
Arguments:
- tokens: bfloat16 [4, 2048, 512], P('dp', ('seq', 'mp')), may hold values from -6 to 6
- segments: int32 [4, 2048], P('dp', ('seq', 'mp')), may hold values from 0 to 16, as said below
- timesteps: int32 [4], P('dp'), may hold values from 0 to 999
- step_table: bfloat16 [1000, 512], replicated, may hold values from -3 to 3
- first_gain: float32 [512], replicated, may hold values from 0.5 to 1.5
- first_shift: float32 [512], replicated, may hold values from -3 to 3
- query_weight: bfloat16 [512, 512], P(None, 'mp'), may hold values from -0.25 to 0.25
- query_bias: bfloat16 [512], P('mp'), may hold values from -3 to 3
- key_weight: bfloat16 [512, 512], P(None, 'mp'), may hold values from -0.25 to 0.25
- value_weight: bfloat16 [512, 512], P(None, 'mp'), may hold values from -0.25 to 0.25
- value_bias: bfloat16 [512], P('mp'), may hold values from -3 to 3
- out_weight: bfloat16 [512, 512], P('mp'), may hold values from -2 to 2
- out_bias: bfloat16 [512], replicated, may hold values from -3 to 3
- second_gain: float32 [512], replicated, may hold values from 0.5 to 1.5
- second_shift: float32 [512], replicated, may hold values from -3 to 3
- up_weight: bfloat16 [512, 2048], P(None, 'mp'), may hold values from -0.25 to 0.25
- up_bias: bfloat16 [2048], P('mp'), may hold values from -3 to 3
- down_weight: bfloat16 [2048, 512], P('mp'), may hold values from -0.25 to 0.25
- down_bias: bfloat16 [512], replicated, may hold values from -3 to 3
- cotangent: bfloat16 [4, 2048, 512], P('dp', ('seq', 'mp')), may hold values from -6 to 6
Outputs:
- result: bfloat16 [4, 2048, 512], P('dp', ('seq', 'mp'))
- token_grad: float32 [4, 2048, 512], P('dp', ('seq', 'mp'))
- table_grad: float32 [1000, 512], replicated
- first_gain_grad: float32 [512], replicated
- first_shift_grad: float32 [512], replicated
- query_weight_grad: float32 [512, 512], P(None, 'mp')
- query_bias_grad: float32 [512], P('mp')
- key_weight_grad: float32 [512, 512], P(None, 'mp')
- value_weight_grad: float32 [512, 512], P(None, 'mp')
- value_bias_grad: float32 [512], P('mp')
- out_weight_grad: float32 [512, 512], P('mp')
- out_bias_grad: float32 [512], replicated
- second_gain_grad: float32 [512], replicated
- second_shift_grad: float32 [512], replicated
- up_weight_grad: float32 [512, 2048], P(None, 'mp')
- up_bias_grad: float32 [2048], P('mp')
- down_weight_grad: float32 [2048, 512], P('mp')
- down_bias_grad: float32 [512], replicated
Inputs may be any that keep to these rules, and one draw needn't show every extreme that they name: `segments`: along each row the ids never fall before the padding; 0 marks padding, which fills the last 32 to 128 characters of every row and nothing else.
All inputs are finite; a program needn't handle non-finite values.
Results may differ from a plain program's by a relative error of at most 0.03.
Values may be sent and summed in bfloat16 or wider, within the bound.
A program may use at most 128 MiB of HBM per device.

v0:
```python
import functools
import math

import jax
import jax.numpy as jnp
from jax import lax
from jax.experimental import pallas as pl
from jax.experimental.pallas import tpu as pltpu
from jax.sharding import PartitionSpec as P

MESH = pl.DeviceIdType.MESH
BF, F32 = jnp.bfloat16, jnp.float32
NN = (((1,), (0,)), ((), ()))
NT = (((1,), (1,)), ((), ()))
TN = (((0,), (0,)), ((), ()))
HEAD_DIM = 64
BLOCK = 128
PAIR = 2 * HEAD_DIM
MASKED = -1e30
GELU_A = 0.044715
GELU_C = math.sqrt(2.0 / math.pi)
OUT_AT, PAIR_AT, PAIR_ROWS, WG_ROWS = 4096, (4608, 5376), 768, 6144
SV_TABLE = 16
RECEIVES, SENDS, KEEPS = 184, 48, 28
SPANS_AT, ROWS_AT = 128, 144
PEERS = ("y", "zl", "diag")
ORDER_A = (("x",), ("y",), ("zl", "zh"))
ORDER_B = (("y",), ("x",), ("zl", "zh"))
ORDER_C = (("zl",), ("x",), ("y",), ("zh",))
WAVE_ONE = ((0, 512, ORDER_A), (512, 512, ORDER_B), (1024, 512, ORDER_C))
WAVE_TWO = ((1536, 512, ORDER_A), (2048, 512, ORDER_B), (2560, 512, ORDER_C))
WAVE_THREE = ((3072, 512, ORDER_A), (3584, 512, ORDER_B), (4096, 512, ORDER_C))
WAVE_PAIR = (((4608, 512, ORDER_A), (5120, 256, ORDER_B)), ((5376, 512, ORDER_A), (5888, 256, ORDER_B)))


def dot(a, b, dims):
    return lax.dot_general(a, b, dims, preferred_element_type=F32)


def bit(v, n):
    return lax.rem(lax.div(v, n), 2)


def flip(v, n):
    return v + n - 2 * n * bit(v, n)


def here():
    return lax.axis_index("dp"), lax.axis_index("seq"), lax.axis_index("mp")


def neighbour(name):
    dp, seq, mp = here()
    dims = {"diag": ("y", "zl")}.get(name, name if isinstance(name, tuple) else (name,))
    for dim in dims:
        if dim == "core":
            mp = 1 - mp
        elif dim == "x":
            dp = 1 - dp
        else:
            seq = flip(seq, {"y": 1, "zl": 2, "zh": 4}[dim])
    return (dp, seq, mp)


def side(name):
    dp, seq, mp = here()
    return {"x": dp, "y": bit(seq, 1), "zl": bit(seq, 2), "zh": bit(seq, 4), "core": mp}[name]


def relations(stage):
    return [tuple(dim for i, dim in enumerate(stage) if k >> i & 1) for k in range(1, 1 << len(stage))]


def rank(stage, differs=()):
    place = 0
    for dim in stage:
        b = side(dim)
        place = 2 * place + (1 - b if dim in differs else b)
    return place


def greet(names):
    barrier = pltpu.get_barrier_semaphore()
    for name in names:
        pl.semaphore_signal(barrier, inc=1, device_id=neighbour(name), device_id_type=MESH)
    pl.semaphore_wait(barrier, len(names))


class Wire:
    def __init__(self, send_sem, recv_sem):
        self.send_sem, self.recv_sem = send_sem, recv_sem
        self.count, self.slots = 0, 0
        self.leaving = {}

    def slot(self):
        self.slots += 1
        return self.slots - 1

    def send(self, src, dst, name, slot=None):
        if slot is None:
            slot = self.slot()
        if slot in self.leaving:
            self.leaving.pop(slot).wait_send()
        copy = pltpu.make_async_remote_copy(
            src_ref=src,
            dst_ref=dst,
            send_sem=self.send_sem.at[slot],
            recv_sem=self.recv_sem.at[self.count],
            device_id=neighbour(name),
            device_id_type=MESH,
        )
        copy.start()
        self.count += 1
        assert self.count <= RECEIVES and slot < SENDS
        self.leaving[slot] = copy
        return copy

    def finish(self):
        for copy in self.leaving.values():
            copy.wait_send()
        self.leaving = {}
        self.slots = 0


def any_spec(n):
    return [pl.BlockSpec(memory_space=pl.ANY)] * n


def vmem_spec(n):
    return [pl.BlockSpec(memory_space=pltpu.VMEM)] * n


def normalise(value):
    centred = value - jnp.mean(value, axis=-1, keepdims=True)
    rstd = lax.rsqrt(jnp.mean(centred * centred, axis=-1, keepdims=True) + 1e-5)
    return centred * rstd, rstd


def normalise_back(grad_hat, hat, rstd):
    return rstd * (
        grad_hat
        - jnp.mean(grad_hat, axis=-1, keepdims=True)
        - hat * jnp.mean(grad_hat * hat, axis=-1, keepdims=True)
    )


def column_sum(value):
    return jnp.sum(value, axis=0, keepdims=True)


class Chains:
    def __init__(self):
        self.queue = []

    def add(self, *chains):
        for chain in chains:
            next(chain)
            self.queue.append(chain)

    def tick(self, n=1):
        for _ in range(min(n, len(self.queue))):
            chain = self.queue.pop(0)
            try:
                next(chain)
                self.queue.append(chain)
            except StopIteration:
                pass

    def drain(self):
        while self.queue:
            self.tick()


def layer_kernel(
    has_x,
    tokens, cot, wq_h, wk_h, wv_h, wo_h, up_h, down_h, table_h,
    segments, timesteps, gain_1, shift_1, gain_2, shift_2, out_bias_1, down_bias_1, query_bias_1, value_bias_1, up_bias_1,
    wg_h, sv_out, tg_out, res_out,
    xrow, xcross, table, cot2, wq, wk, wv, wo, up, down, bias,
    normed, normed_t, k_ref, v_ref, hot, s_buf, att, att_t, lse, q_ref, dkv, dq_ref, t_buf, part_top, part_sum,
    wg, acc, core_buf, step_buf, wg_out, t_out, t_core, t_acc, t_step, result2, sv_buf, sv_acc,
    send_sem, recv_sem, local_sem,
):
    dp, seq, mp = here()
    g = lax.div(seq, 4)
    pseq = flip(seq, 4)
    own, par = 2 * seq + mp, 2 * pseq + mp
    y, zl = bit(seq, 1), bit(seq, 2)
    d = normed.shape[1]
    length = normed.shape[0]
    pairs = d // PAIR
    step = 512
    steps = length // step
    nb = step // BLOCK
    ff = up.shape[1]
    half = ff // 2
    nq = 2 * BLOCK
    wire = Wire(send_sem, recv_sem)
    chains = Chains()
    kept = []

    def keep(src, dst):
        copy = pltpu.make_async_copy(src, dst, local_sem.at[len(kept)])
        copy.start()
        kept.append(copy)
        return copy

    def columns(ref):
        w = ref.shape[1] // 2
        return ref.at[:, pl.ds(pl.multiple_of(mp * w, w), w)]

    def rows(ref):
        w = ref.shape[0] // 2
        return ref.at[pl.ds(pl.multiple_of(mp * w, w), w)]

    def arrive(copies):
        for copy in copies:
            copy.wait_recv()

    chars = pl.ds(0, BLOCK)
    cross_kept = keep(tokens.at[1 - g], xcross.at[chars])
    own_kept = keep(tokens.at[g], xrow.at[own, chars])
    early_kept = [keep(table_h, table), keep(wk_h, columns(wk)), keep(wv_h, columns(wv)), keep(wq_h, columns(wq))]
    spans = segments[...].astype(F32)
    first_row = jnp.where(g == 0, spans[0:1, :], spans[1:2, :])
    second_row = jnp.where(g == 0, spans[1:2, :], spans[0:1, :])
    blank = jnp.zeros((ROWS_AT - SPANS_AT, d - BLOCK), F32)

    def span_rows(row):
        return jnp.concatenate([jnp.broadcast_to(row, (ROWS_AT - SPANS_AT, BLOCK)), blank], axis=1).astype(BF)

    xcross[SPANS_AT:, :] = span_rows(second_row)
    xrow[own, SPANS_AT:, :] = span_rows(first_row)

    def line(ref):
        return ref[...].astype(F32).reshape(1, ref.shape[0])

    bias[mp] = jnp.concatenate(
        [jnp.concatenate([line(query_bias_1), line(value_bias_1)], axis=1)]
        + [line(up_bias_1)[:, i * d : (i + 1) * d] for i in range(half // d)]
        + [jnp.zeros((8 - 1 - half // d, d), F32)],
        axis=0,
    )
    greet(("core", "y", "zl", "diag", "zh", ("zl", "zh")) + (("x", ("x", "y")) if has_x else ()))

    upper, lower = pl.ds(0, BLOCK // 2), pl.ds(BLOCK // 2, ROWS_AT - BLOCK // 2)
    cross_kept.wait()
    crossing = [wire.send(xcross.at[part], xrow.at[own, part], "zh") for part in (upper, lower)]
    own_kept.wait()
    first = {"y": wire.send(xrow.at[own], xrow.at[own], "y")}
    own_mate = wire.send(xrow.at[own], xrow.at[own], "core")
    early = [
        wire.send(wk_h, columns(wk), "core"),
        wire.send(wv_h, columns(wv), "core"),
        wire.send(wq_h, columns(wq), "core"),
        wire.send(bias.at[mp], bias.at[mp], "core"),
    ]
    late_kept = [
        keep(src, dst)
        for src, dst in ((wo_h, rows(wo)), (up_h, columns(up)), (down_h, rows(down)), (cot.at[g], cot2.at[0]))
    ]
    for copy in early_kept:
        copy.wait()

    t_buf[...] = jnp.zeros_like(t_buf)

    lane = lax.broadcasted_iota(jnp.int32, timesteps.shape, 1)
    moment = jnp.sum(jnp.where(lane == g, timesteps[...], 0).astype(F32), axis=1, keepdims=True)
    ids = lax.broadcasted_iota(jnp.int32, (8, table.shape[0]), 1).astype(F32)
    row_embed = dot(jnp.where(ids == moment, 1.0, 0.0).astype(BF), table[...], NN)[0:1, :]
    gain, shift = line(gain_1), line(shift_1)

    def hidden_of(block):
        return block.astype(F32) + row_embed

    def seg_column(b):
        return jnp.transpose(xrow[b, SPANS_AT:, 0:BLOCK].astype(F32))[:, 0:1]

    arrive(early)
    query_bias = jnp.concatenate([bias[0, 0:1, :256], bias[1, 0:1, :256]], axis=1)
    value_bias = jnp.concatenate([bias[0, 0:1, 256:], bias[1, 0:1, 256:]], axis=1)

    def project(s):
        n = 2 * BLOCK
        at = pl.ds(pl.multiple_of(s * n, n), n)
        hat, _ = normalise(hidden_of(xrow[pl.ds(2 * s, 2), 0:BLOCK, :].reshape(n, d)))
        low = (hat * gain + shift).astype(BF)
        normed[at, :] = low
        normed_t[:, at] = jnp.transpose(low)
        k_ref[at, :] = dot(low, wk[...], NN).astype(BF)
        v_ref[at, :] = (dot(low, wv[...], NN) + value_bias).astype(BF)
        spans = jnp.concatenate([seg_column(2 * s + i) for i in range(2)], axis=0)
        lanes = lax.broadcasted_iota(jnp.int32, (n, BLOCK), 1).astype(F32)
        hot[at, :] = jnp.where(spans == lanes, 1.0, 0.0).astype(BF)

    def beyond(base, name):
        return {"y": flip(base, 1), "zl": flip(base, 2), "diag": flip(flip(base, 1), 2)}[name]

    def to_mate(s):
        block = xrow.at[2 * s + mp]
        return wire.send(block, block, "core")

    own_mate.wait_recv()
    project(seq)
    for name in ("zl", "diag"):
        first[name] = wire.send(xrow.at[own], xrow.at[own], name)
    first["y"].wait_recv()
    mates = {"y": to_mate(beyond(seq, "y"))}
    second = {name: [] for name in PEERS}
    for copy, part in zip(crossing, (upper, lower)):
        copy.wait_recv()
        for name in PEERS:
            second[name].append(wire.send(xrow.at[par, part], xrow.at[par, part], name))
    par_mate = to_mate(pseq)
    mates["y"].wait_recv()
    project(beyond(seq, "y"))
    for name in ("zl", "diag"):
        first[name].wait_recv()
        mates[name] = to_mate(beyond(seq, name))
    late = [
        wire.send(src, dst, "core")
        for src, dst in ((wo_h, rows(wo)), (up_h, columns(up)), (down_h, rows(down)))
    ]
    late.append(wire.send(cot.at[1 - g], cot2.at[1], "zh"))
    par_mate.wait_recv()
    project(pseq)

    def query_rows(ref):
        return jnp.concatenate(
            [ref[pl.ds(pl.multiple_of(b * BLOCK, BLOCK), BLOCK), :] for b in (own, par)], axis=0
        )

    scale = 1.0 / math.sqrt(HEAD_DIM)
    query_low = (dot(query_rows(normed), wq[...], NN) + query_bias).astype(BF)
    q_ref[...] = (query_low.astype(F32) * scale).astype(BF)
    for name in ("zl", "diag"):
        mates[name].wait_recv()
        project(beyond(seq, name))

    spans_q = jnp.concatenate([seg_column(own), seg_column(par)], axis=0)
    lanes_q = lax.broadcasted_iota(jnp.int32, (nq, BLOCK), 1).astype(F32)
    other = jnp.where(spans_q == lanes_q, 0.0, MASKED).astype(BF)
    live = jnp.where(spans_q > 0.0, 1.0, 0.0)
    other2 = jnp.concatenate([other, other], axis=0)
    first_head = lax.broadcasted_iota(jnp.int32, (nq, PAIR), 1) < HEAD_DIM
    first_head_t = lax.broadcasted_iota(jnp.int32, (PAIR, nq), 0) < HEAD_DIM

    def split_heads(value):
        wide = value.astype(F32)
        return jnp.concatenate(
            [jnp.where(first_head, wide, 0.0), jnp.where(first_head, 0.0, wide)], axis=0
        ).astype(BF)

    def join_heads_t(value):
        return jnp.where(first_head_t, value[:, :nq], value[:, nq:])

    def lanes_of(p):
        return pl.ds(p * PAIR if isinstance(p, int) else pl.multiple_of(p * PAIR, PAIR), PAIR)

    def chunk(c):
        return pl.ds(c * step, step)

    def attend(p, places):
        at = lanes_of(p)
        query = jnp.concatenate([split_heads(q_ref[:, at]), other2], axis=1)
        top = jnp.full((8, 2 * nq), -3e38, F32)
        keys_at = [pl.ds(pl.multiple_of(s * nq, nq), nq) for s in places]
        for i, here_at in enumerate(keys_at):
            keys = jnp.concatenate([k_ref[here_at, at], hot[here_at, :]], axis=1)
            scores = dot(keys, query, NT)
            s_buf[pl.ds(i * nq, nq), :] = scores
            top = jnp.maximum(top, jnp.max(scores.reshape(nq // 8, 8, 2 * nq), axis=0))
        top = jnp.max(top, axis=0, keepdims=True)
        total = jnp.zeros((8, 2 * nq), F32)
        summed = jnp.zeros((PAIR, 2 * nq), F32)
        for i, here_at in enumerate(keys_at):
            weights = jnp.exp(s_buf[pl.ds(i * nq, nq), :] - top)
            total = total + jnp.sum(weights.reshape(nq // 8, 8, 2 * nq), axis=0)
            summed = summed + dot(v_ref[here_at, at], weights.astype(BF), TN)
        return top, jnp.sum(total, axis=0, keepdims=True), summed

    near = [seq] + [beyond(seq, name) for name in PEERS] + [pseq]
    def near_pair(p, carry):
        top, total, summed = attend(p, near)
        part_top[p, 0:1, :] = top
        part_top[p, 8:9, :] = total
        part_sum[p] = summed
        return carry

    lax.fori_loop(0, pairs, near_pair, 0)
    for name in PEERS:
        arrive(second[name])
        mates[name] = to_mate(beyond(pseq, name))
    for name in PEERS:
        mates[name].wait_recv()
        project(beyond(pseq, name))
    far = [beyond(pseq, name) for name in PEERS]
    def far_pair(p, carry):
        top, total, summed = attend(p, far)
        top_near = part_top[p, 0:1, :]
        top_all = jnp.maximum(top, top_near)
        weight, weight_near = jnp.exp(top - top_all), jnp.exp(top_near - top_all)
        total = total * weight + part_top[p, 8:9, :] * weight_near
        summed = summed * weight + part_sum[p] * weight_near
        joined = join_heads_t(summed / total)
        att_t[p] = joined
        att[:, lanes_of(p)] = jnp.transpose(joined)
        lse[p] = jnp.broadcast_to(top_all + jnp.log(total), (8, 2 * nq))
        return carry

    lax.fori_loop(0, pairs, far_pair, 0)

    for copy in late_kept:
        copy.wait()
    arrive(late)
    wire.finish()

    def stages_of(order):
        stages = [tuple(dim for dim in stage if has_x or dim != "x") for stage in order]
        return [stage for stage in stages if stage]

    def add_rows(out, out_at, terms, n):
        size = next(s for s in (256, 192, 128, 96, 64, 48, 32, 16) if n % s == 0)

        def one(i, carry):
            def at(base):
                return pl.ds(pl.multiple_of(base + i * size, size), size)

            values = [ref[at(base), :] for ref, base in terms]
            if len(values) == 2:
                out[at(out_at), :] = values[0] + values[1]
            else:
                out[at(out_at), :] = sum(value.astype(F32) for value in values).astype(BF)
            return carry

        lax.fori_loop(0, n // size, one, 0)

    def weights_chain(low, size, order):
        stages = stages_of(order)
        whole = pl.ds(low, size)
        used = low
        slots = [wire.slot() for _ in range(max(len(relations(stage)) for stage in stages))]
        copy = wire.send(wg.at[1 - mp, whole], core_buf.at[whole], "core", slots[0])
        yield
        copy.wait_recv()
        add_rows(acc, low, [(wg.at[mp], low), (core_buf, low)], size)
        for i, stage in enumerate(stages):
            size = size >> len(stage)
            terms, copies = [], []
            for slot, differs in zip(slots, relations(stage)):
                there = pl.ds(pl.multiple_of(low + rank(stage, differs) * size, size), size)
                copies.append(wire.send(acc.at[there], step_buf.at[pl.ds(used, size)], differs, slot))
                terms.append((step_buf, used))
                used += size
            yield
            arrive(copies)
            low = low + rank(stage) * size
            add_rows(wg_out if i == len(stages) - 1 else acc, low, [(acc, low)] + terms, size)
        for stage in reversed(stages):
            at = pl.ds(pl.multiple_of(low, size), size)
            copies = [wire.send(wg_out.at[at], wg_out.at[at], differs, slot) for slot, differs in zip(slots, relations(stage))]
            yield
            arrive(copies)
            low = low - rank(stage) * size
            size = size << len(stage)
        keep(wg_out.at[whole], wg_h.at[whole])

    def start_weights(wave):
        chains.add(*[weights_chain(low, size, order) for low, size, order in wave])

    finished = len(kept)
    mixed = (att[...] * live).astype(BF)
    hidden_q = hidden_of(jnp.concatenate([xrow[own, 0:BLOCK, :], xrow[par, 0:BLOCK, :]], axis=0))
    residual = hidden_q + dot(mixed, wo[...], NN) + line(out_bias_1)
    gain2, shift2 = line(gain_2), line(shift_2)
    hat2, rstd2 = normalise(residual)
    normed2 = (hat2 * gain2 + shift2).astype(BF)
    cotangent = jnp.concatenate([cot2[0], cot2[1]], axis=0)
    unit_result = residual + line(down_bias_1)
    grad_normed2 = jnp.zeros((nq, d), F32)
    sv = sv_acc.at[0]
    for r in range(half // step):
        for m in range(2):
            j = (m * half + r * step) // step
            units = pl.ds(j * step, step)
            inner = dot(normed2, up[:, units], NN) + bias[m, 1 + r : 2 + r, :]
            square = inner * inner
            bent = jnp.tanh(GELU_C * inner * (1.0 + GELU_A * square))
            activated = (0.5 * inner * (1.0 + bent)).astype(BF)
            unit_result = unit_result + dot(activated, down[units, :], NN)
            slope = 0.5 * (1.0 + bent) + 0.5 * inner * (1.0 - bent * bent) * (
                GELU_C * (1.0 + 3.0 * GELU_A * square)
            )
            grad_inner = (dot(cotangent, down[units, :], NT) * slope).astype(BF)
            grad_normed2 = grad_normed2 + dot(grad_inner, up[:, units], NT)
            down_grad = dot(activated, cotangent, TN).astype(BF)
            up_grad = dot(normed2, grad_inner, TN).astype(BF)
            for b in range(2):
                at = slice(b * 256, (b + 1) * 256)
                wg[m, pl.ds(2048 * r + b * 512, 512), :] = up_grad[:, at]
                wg[m, pl.ds(2048 * r + 1024 + b * 512, 512), :] = down_grad[:, at]
            sv[6 + j : 7 + j, :] = column_sum(grad_inner.astype(F32))
        start_weights((WAVE_ONE, WAVE_TWO)[r])
        chains.tick(3 * r)
    out = unit_result.astype(BF)
    result2[0] = out[:BLOCK]
    result2[1] = out[BLOCK:]
    result_back = wire.send(result2.at[1], res_out.at[g], "zh")
    res_out[g] = out[:BLOCK]
    cot_f = cotangent.astype(F32)
    grad_residual = cot_f + normalise_back(grad_normed2 * gain2, hat2, rstd2)
    sv[2:3, :] = column_sum(grad_normed2 * hat2)
    sv[3:4, :] = column_sum(grad_normed2)
    sv[4:5, :] = column_sum(grad_residual)
    sv[5:6, :] = column_sum(cot_f)
    branch_grad = grad_residual.astype(BF)
    out_grad = dot(mixed, branch_grad, TN).astype(BF)
    for m in range(2):
        for b in range(2):
            wg[m, pl.ds(OUT_AT + b * 256, 256), :] = out_grad[m * 256 : (m + 1) * 256, b * 256 : (b + 1) * 256]
    start_weights(WAVE_THREE)
    att[...] = dot(branch_grad, wo[...], NT).astype(BF).astype(F32) * live

    def back(p):
        at = lanes_of(p)
        query = split_heads(q_ref[:, at])
        query_wide = jnp.concatenate([query, other2], axis=1)
        heads = att[:, at]
        grads = split_heads(heads)
        product = jnp.transpose(heads) * att_t[p]
        delta = jnp.concatenate([column_sum(product[:HEAD_DIM]), column_sum(product[HEAD_DIM:])], axis=1)
        log_total = lse[p][0:1, :]
        query_grad = jnp.zeros((PAIR, 2 * nq), F32)
        for c in range(steps):
            keys = k_ref[chunk(c), at]
            scores = dot(jnp.concatenate([keys, hot[chunk(c), :]], axis=1), query_wide, NT)
            probs = jnp.exp(scores - log_total)
            grad_probs = dot(v_ref[chunk(c), at], grads, NT)
            grad_scores = (probs * (grad_probs - delta)).astype(BF)
            dkv[p, chunk(c), 0:PAIR] = dot(grad_scores, query, NN).astype(BF)
            dkv[p, chunk(c), PAIR:] = dot(probs.astype(BF), grads, NN).astype(BF)
            query_grad = query_grad + dot(keys, grad_scores, TN)
            chains.tick(2)
        joined = join_heads_t(query_grad) * scale
        dq_ref[:, at] = jnp.transpose(joined).astype(BF)

    normed_q = query_rows(normed)
    for n in range(2):
        for m in range(2):
            back(2 * m + n)
        for m in range(2):
            p = 2 * m + n
            pair_grad = dot(normed_t[...], dkv[p], NN)
            wg[m, pl.ds(PAIR_AT[n], d), :] = pair_grad.astype(BF)
            pair_grad = dot(normed_q, dq_ref[:, lanes_of(p)], TN).astype(BF)
            wg[m, pl.ds(PAIR_AT[n] + d, d // 2), 0:PAIR] = pair_grad[: d // 2]
            wg[m, pl.ds(PAIR_AT[n] + d, d // 2), PAIR:] = pair_grad[d // 2 :]
        start_weights(WAVE_PAIR[n])

    def tokens_back(grad_normed, block):
        hat, rstd = normalise(hidden_of(block))
        return (
            normalise_back(grad_normed * gain, hat, rstd),
            column_sum(grad_normed * hat),
            column_sum(grad_normed),
        )

    query_grad = dq_ref[...]
    token_grad, gain_sum, shift_sum = tokens_back(
        dot(query_grad, wq[...], NT), jnp.concatenate([xrow[own, 0:BLOCK, :], xrow[par, 0:BLOCK, :]], axis=0)
    )
    token_grad = token_grad + grad_residual
    t_buf[own] = token_grad[:BLOCK]
    t_buf[par] = token_grad[BLOCK:]
    token_sum = column_sum(token_grad)
    value_sums = [jnp.zeros((1, PAIR), F32) for _ in range(pairs)]

    def tokens_chain(hi, dims):
        slot = wire.slot()
        one, two = dims
        copy = wire.send(t_out.at[hi, :, :, 1 - mp], t_core.at[hi], "core", slot)
        yield
        copy.wait_recv()
        for b in range(2):
            for c in range(2):
                t_acc[hi, b, c] = t_out[hi, b, c, mp] + t_core[hi, b, c]
        if one == "y":
            copy = wire.send(t_acc.at[hi, :, 1 - y], t_step.at[hi, 0:2], "y", slot)
        else:
            copy = wire.send(t_acc.at[hi, 1 - zl], t_step.at[hi, 0:2], "zl", slot)
        yield
        copy.wait_recv()
        if one == "y":
            for i in range(2):
                t_acc[hi, i, y] += t_step[hi, i]
            copy = wire.send(t_acc.at[hi, 1 - zl, y], t_step.at[hi, 2], "zl", slot)
        else:
            for i in range(2):
                t_acc[hi, zl, i] += t_step[hi, i]
            copy = wire.send(t_acc.at[hi, zl, 1 - y], t_step.at[hi, 2], "y", slot)
        yield
        copy.wait_recv()
        t_acc[hi, zl, y] += t_step[hi, 2]
        if two == "zl":
            copy = wire.send(t_acc.at[hi, zl, y], tg_out.at[g], "zh", slot)
            yield
            copy.wait_recv()
        else:
            tg_out[g] = t_acc[hi, zl, y]

    for hi, dims in ((1 - g, ("y", "zl")), (g, ("zl", "y"))):
        for c in range(2):
            place = 2 * hi + c
            at = pl.ds(pl.multiple_of(place * step, step), step)
            grad_normed = jnp.zeros((step, d), F32)
            for p in range(pairs):
                pair_grad = dkv[p, at, :]
                both = jnp.concatenate([wk[:, lanes_of(p)], wv[:, lanes_of(p)]], axis=1)
                grad_normed = grad_normed + dot(pair_grad, both, NT)
                value_sums[p] = value_sums[p] + column_sum(pair_grad[:, PAIR:].astype(F32))
            blocks_at = pl.ds(place * nb, nb)
            token_grad, a, b = tokens_back(grad_normed, xrow[blocks_at, 0:BLOCK, :].reshape(step, d))
            gain_sum, shift_sum, token_sum = gain_sum + a, shift_sum + b, token_sum + column_sum(token_grad)
            token_grad = t_buf[blocks_at] + token_grad.reshape(nb, BLOCK, d)
            for i in range(nb):
                t_out[hi, c, i // 2, i % 2] = token_grad[i].astype(BF)
            chains.tick()
        chains.add(tokens_chain(hi, dims))
    value_sum = jnp.concatenate(value_sums, axis=1)

    sv[0:1, :] = gain_sum
    sv[1:2, :] = shift_sum
    sv[10:11, :] = column_sum(query_grad.astype(F32))
    sv[11:12, :] = value_sum
    sv[12:16, :] = jnp.zeros((4, d), F32)
    slot_lane = lax.broadcasted_iota(jnp.int32, (1, d), 1)
    speaks = jnp.logical_and(lax.rem(seq, 4) == 0, mp == 0)
    my_slot = 2 * dp + g
    sv[12:13, :] = jnp.where(slot_lane == jnp.where(speaks, my_slot, -1), moment, 0.0)
    slot = lax.broadcasted_iota(jnp.int32, (sv.shape[0] - SV_TABLE, d), 0) == my_slot
    sv[SV_TABLE:, :] = jnp.where(slot, token_sum, 0.0)

    def vectors_chain():
        slots = [wire.slot() for _ in range(3)]
        stages = [("core",)] + stages_of((("x", "y"), ("zl", "zh")))
        for i, stage in enumerate(stages):
            copies = [
                wire.send(sv_acc.at[i], sv_buf.at[i, k], differs, slots[k])
                for k, differs in enumerate(relations(stage))
            ]
            yield
            arrive(copies)
            total = sv_acc[i] + sv_buf[i, 0]
            if len(copies) == 3:
                total = total + (sv_buf[i, 1] + sv_buf[i, 2])
            sv_acc[i + 1] = total
        sv_out[...] = sv_acc[len(stages)]
        result_back.wait_recv()

    chains.add(vectors_chain())
    chains.drain()
    wire.finish()
    for copy in kept[finished:]:
        copy.wait()


def layer(big, small, has_x, sv_rows):
    shape = jax.ShapeDtypeStruct
    tokens, up, table = big[0], big[6], big[8]
    d = tokens.shape[2]
    blocks = 2 * lax.axis_size("seq")
    length = blocks * BLOCK
    nq = 2 * BLOCK
    pairs = d // PAIR
    ff = 2 * up.shape[1]
    block = (BLOCK, d)
    vmem = pltpu.VMEM
    return pl.pallas_call(
        functools.partial(layer_kernel, has_x),
        out_shape=(
            shape((WG_ROWS, 256), BF),
            shape((sv_rows, d), F32),
            shape(tokens.shape, BF),
            shape(tokens.shape, BF),
        ),
        in_specs=any_spec(len(big)) + vmem_spec(len(small)),
        out_specs=tuple(any_spec(1) + vmem_spec(3)),
        scratch_shapes=[
            vmem((blocks, ROWS_AT, d), BF),
            vmem((ROWS_AT, d), BF),
            vmem(table.shape, BF),
            vmem((2,) + block, BF),
            vmem((d, d), BF),
            vmem((d, d), BF),
            vmem((d, d), BF),
            vmem((d, d), BF),
            vmem((d, ff), BF),
            vmem((ff, d), BF),
            vmem((2, 8, d), F32),
            vmem((length, d), BF),
            vmem((d, length), BF),
            vmem((length, d), BF),
            vmem((length, d), BF),
            vmem((length, BLOCK), BF),
            vmem((5 * nq, 2 * nq), F32),
            vmem((nq, d), F32),
            vmem((pairs, PAIR, nq), F32),
            vmem((pairs, 8, 2 * nq), F32),
            vmem((nq, d), BF),
            vmem((pairs, length, 2 * PAIR), BF),
            vmem((nq, d), BF),
            vmem((blocks,) + block, F32),
            vmem((pairs, 16, 2 * nq), F32),
            vmem((pairs, PAIR, 2 * nq), F32),
            vmem((2, WG_ROWS, 256), BF),
            vmem((WG_ROWS, 256), BF),
            vmem((WG_ROWS, 256), BF),
            vmem((WG_ROWS, 256), BF),
            vmem((WG_ROWS, 256), BF),
            vmem((2, 2, 2, 2) + block, BF),
            vmem((2, 2, 2) + block, BF),
            vmem((2, 2, 2) + block, BF),
            vmem((2, 3) + block, BF),
            vmem((2,) + block, BF),
            vmem((3, 3, sv_rows, d), F32),
            vmem((4, sv_rows, d), F32),
            pltpu.SemaphoreType.DMA((SENDS,)),
            pltpu.SemaphoreType.DMA((RECEIVES,)),
            pltpu.SemaphoreType.DMA((KEEPS,)),
        ],
        compiler_params=pltpu.CompilerParams(
            collective_id=0, has_side_effects=True, vmem_limit_bytes=62 << 20
        ),
        name="layer",
    )(*big, *small)


def finish_kernel(
    table_rows, wg, tg, res, sv,
    res_o, tg_o, table_o, wq_o, wk_o, wv_o, wo_o, up_o, down_o,
    gain_1, shift_1, query_bias, value_bias, out_bias, gain_2, shift_2, up_bias, down_bias,
    wg_v, tg_v, res_v, tg_f, table_v, wq_v, wk_v, wv_v, wo_v, up_v, down_v,
    in_sem, out_sem,
):
    mp = lax.axis_index("mp")
    leaving = []
    rows = 1024
    parts = WG_ROWS // rows

    def fetch(src, dst, n):
        copy = pltpu.make_async_copy(src, dst, in_sem.at[n])
        copy.start()
        return copy

    def leave(src, dst):
        copy = pltpu.make_async_copy(src, dst, out_sem.at[len(leaving)])
        copy.start()
        leaving.append(copy)

    coming = [fetch(wg.at[pl.ds(i * rows, rows)], wg_v.at[pl.ds(i * rows, rows)], i) for i in range(parts)]
    coming_tg, coming_res = fetch(tg, tg_v, parts), fetch(res, res_v, parts + 1)
    ids = sv[12:13, 0:128]
    spread = jnp.where(lax.broadcasted_iota(jnp.int32, (table_v.shape[0], 128), 0).astype(F32) == ids, 1.0, 0.0)
    sums = jnp.concatenate([sv[SV_TABLE:, :], jnp.zeros((128 - (sv.shape[0] - SV_TABLE), sv.shape[1]), F32)], axis=0)
    table_v[...] = lax.dot_general(spread, sums, NN, precision=lax.Precision.HIGHEST, preferred_element_type=F32)
    leave(table_v, table_o)

    def flat(ref, value):
        ref[...] = value.reshape(ref.shape)

    for ref, r in ((gain_1, 0), (shift_1, 1), (gain_2, 2), (shift_2, 3), (out_bias, 4), (down_bias, 5)):
        flat(ref, sv[r : r + 1, :])
    for ref, r in ((query_bias, 10), (value_bias, 11)):
        flat(ref, jnp.where(mp == 0, sv[r : r + 1, 0:256], sv[r : r + 1, 256:512]))
    flat(up_bias, jnp.where(mp == 0, jnp.concatenate([sv[6:7, :], sv[7:8, :]], axis=1), jnp.concatenate([sv[8:9, :], sv[9:10, :]], axis=1)))

    def take(at, n):
        return wg_v[at : at + n, :].astype(F32)

    for i in range(parts):
        coming[i].wait()
        if i in (0, 2):
            for b in range(2):
                up_v[:, i * 256 + b * 256 : i * 256 + (b + 1) * 256] = take(i * rows + b * 512, 512)
            leave(up_v.at[:, pl.ds(i * 256, 512)], up_o.at[:, pl.ds(i * 256, 512)])
        elif i in (1, 3):
            at = pl.ds(i // 2 * 512, 512)
            for b in range(2):
                down_v[at, b * 256 : (b + 1) * 256] = take(i * rows + b * 512, 512)
            leave(down_v.at[at], down_o.at[at])
        elif i == 4:
            for b in range(2):
                wo_v[:, b * 256 : (b + 1) * 256] = take(OUT_AT + b * 256, 256)
            leave(wo_v, wo_o)
        else:
            for n, at in enumerate(PAIR_AT):
                lanes = slice(n * PAIR, (n + 1) * PAIR)
                both, query = take(at, 512), take(at + 512, 256)
                wk_v[:, lanes] = both[:, :PAIR]
                wv_v[:, lanes] = both[:, PAIR:]
                wq_v[0:256, lanes] = query[:, :PAIR]
                wq_v[256:512, lanes] = query[:, PAIR:]
            leave(wk_v, wk_o)
            leave(wv_v, wv_o)
            leave(wq_v, wq_o)
    coming_res.wait()
    leave(res_v, res_o)
    coming_tg.wait()
    tg_f[...] = tg_v[...].astype(F32)
    leave(tg_f, tg_o)
    for copy in leaving:
        copy.wait()


def finish(wg, tg, res, sv, table_rows, steps, units):
    shape = jax.ShapeDtypeStruct
    d = sv.shape[1]
    big = [
        shape(res.shape, BF), shape(tg.shape, F32), shape((steps, d), F32),
        shape((d, d // 2), F32), shape((d, d // 2), F32), shape((d, d // 2), F32), shape((d // 2, d), F32),
        shape((d, units), F32), shape((units, d), F32),
    ]
    small = [shape((n,), F32) for n in (d, d, d // 2, d // 2, d, d, d, units, d)]
    vmem = pltpu.VMEM
    return pl.pallas_call(
        functools.partial(finish_kernel, table_rows),
        out_shape=tuple(big + small),
        in_specs=any_spec(3) + vmem_spec(1),
        out_specs=tuple(any_spec(len(big)) + vmem_spec(len(small))),
        scratch_shapes=[vmem(wg.shape, BF), vmem(tg.shape, BF), vmem(res.shape, BF), vmem(tg.shape, F32)]
        + [vmem(item.shape, F32) for item in big[2:]]
        + [pltpu.SemaphoreType.DMA((8,)), pltpu.SemaphoreType.DMA((12,))],
        compiler_params=pltpu.CompilerParams(vmem_limit_bytes=62 << 20),
        name="finish",
    )(wg, tg, res, sv)


def local(
    n_dp, tokens, segments, timesteps, step_table, first_gain, first_shift, query_weight, query_bias,
    key_weight, value_weight, value_bias, out_weight, out_bias, second_gain, second_shift,
    up_weight, up_bias, down_weight, down_bias, cotangent,
):
    table_rows = tokens.shape[0] * n_dp
    sv_rows = SV_TABLE + -(-table_rows // 8) * 8
    wg, sv, token_grad, result = layer(
        (tokens, cotangent, query_weight, key_weight, value_weight, out_weight, up_weight, down_weight, step_table),
        (segments, timesteps[None, :], first_gain, first_shift, second_gain, second_shift, out_bias, down_bias,
         query_bias, value_bias, up_bias),
        n_dp == 2, sv_rows,
    )
    if n_dp != 2:
        wg, sv = lax.psum((wg, sv), "dp")
    (result, token_grad, table_grad, wq, wk, wv, wo, up, down,
     gain_1, shift_1, bq, bv, bo, gain_2, shift_2, bu, bd) = finish(
        wg, token_grad, result, sv, table_rows, step_table.shape[0], up_weight.shape[1]
    )
    return (
        result, token_grad, table_grad, gain_1, shift_1, wq, bq, wk, wv, bv, wo, bo, gain_2, shift_2, up, bu, down, bd
    )


def solution(mesh):
    rows, chars, whole = P("dp", ("seq", "mp"), None), P("dp", ("seq", "mp")), P()
    columns, split, tall = P(None, "mp"), P("mp"), P("mp", None)
    in_specs = (
        rows, chars, P("dp"), whole, whole, whole, columns, split, columns, columns, split, tall,
        whole, whole, whole, columns, split, tall, whole, rows,
    )
    out_specs = (
        rows, rows, whole, whole, whole, columns, split, columns, columns, split, tall,
        whole, whole, whole, columns, split, tall, whole,
    )
    return jax.shard_map(
        functools.partial(local, mesh.shape["dp"]),
        mesh=mesh,
        in_specs=in_specs,
        out_specs=out_specs,
        check_vma=False,
    )
```

profile of v0, /device:TPU:0, one launch (start us, length us, event | category | flops | bytes accessed | tf_op | source)
XLA Modules:
  0.0 129.1 jit_solution(6854000177842268097)
XLA Ops:
  0.7 121.4 %layer.1 = (bf16[6144,256]{1,0:T(8,128)(2,1)}, f32[24,512]{1,0:T(8,128)}, bf16[2,128,512]{2,1,0:T(8,128)(2,1)}, bf16[2,128,512]{2,1,0:T(8,128)(2,1)}) custom-call(bf16[2,128,512]{2,1,0:T(8,128)(2,1)} %tokens.1, bf16[2,128,512]{2,1,0:T(8,128)(2,1)} %cot.1, bf16[512,256]{1,0:T(8,128)(2,1)} %wq_h.1, bf16[512,256]{1,0:T(8,128)(2,1)} %wk_h.1, ...), custom_call_target="tpu_custom_call" | custom-call | tf_op jit(solution)/shard_map/layer/pallas_call | solution.py:678
  122.1 6.9 %finish.1 = (bf16[2,128,512]{2,1,0:T(8,128)(2,1)}, f32[2,128,512]{2,1,0:T(8,128)}, f32[1000,512]{1,0:T(8,128)}, f32[512,256]{1,0:T(8,128)}, f32[512,256]{1,0:T(8...) custom-call(bf16[6144,256]{1,0:T(8,128)(2,1)} %get-tuple-element.40., ...), custom_call_target="tpu_custom_call" | custom-call | tf_op jit(solution)/shard_map/finish/pallas_call | solution.py:825
where the time goes:
time: 129 us
  Pallas kernels  128 us (99%)
    pallas_call x1, Pallas kernels, layer(): pl.pallas_call(functools.partial(layer_kernel, has_x), out_shape=(shape((...  121 us
    pallas_call x1, Pallas kernels, finish(): pl.pallas_call(functools.partial(finish_kernel, table_rows), out_shape=tu...  6.86 us

commit v1 on v0

--- a/solution.py
+++ b/solution.py
@@ -21,16 +21,61 @@
 GELU_C = math.sqrt(2.0 / math.pi)
 OUT_AT, PAIR_AT, PAIR_ROWS, WG_ROWS = 4096, (4608, 5376), 768, 6144
 SV_TABLE = 16
-RECEIVES, SENDS, KEEPS = 184, 48, 28
+RECEIVES, SENDS, KEEPS = 132, 48, 30
 SPANS_AT, ROWS_AT = 128, 144
 PEERS = ("y", "zl", "diag")
-ORDER_A = (("x",), ("y",), ("zl", "zh"))
-ORDER_B = (("y",), ("x",), ("zl", "zh"))
-ORDER_C = (("zl",), ("x",), ("y",), ("zh",))
-WAVE_ONE = ((0, 512, ORDER_A), (512, 512, ORDER_B), (1024, 512, ORDER_C))
-WAVE_TWO = ((1536, 512, ORDER_A), (2048, 512, ORDER_B), (2560, 512, ORDER_C))
-WAVE_THREE = ((3072, 512, ORDER_A), (3584, 512, ORDER_B), (4096, 512, ORDER_C))
-WAVE_PAIR = (((4608, 512, ORDER_A), (5120, 256, ORDER_B)), ((5376, 512, ORDER_A), (5888, 256, ORDER_B)))
+PARTS = {
+    "a": (
+        ("a0", 0, 768, (("zl",), ("x", "y",), ("zh",),)),
+        ("a1", 768, 768, (("x",), ("y",), ("zl", "zh",),)),
+    ),
+    "b": (
+        ("b0", 1536, 768, (("x",), ("y",), ("zl", "zh",),)),
+        ("b1", 2304, 768, (("x", "y",), ("zl", "zh",),)),
+    ),
+    "c": (
+        ("c0", 3072, 768, (("x",), ("zl", "zh",), ("y",),)),
+        ("c1", 3840, 768, (("y",), ("x",), ("zl",), ("zh",),)),
+    ),
+    "p": (
+        ("p0", 4608, 768, (("x",), ("y",), ("zl", "zh",),)),
+    ),
+    "q": (
+        ("q0", 5376, 768, (("x", "y",), ("zl", "zh",),)),
+    ),
+}
+SCRIPT = (
+    (),
+    ("a0", "a1", "b0", "b1",),
+    (),
+    (),
+    ("a0", "a1", "c0", "c1",),
+    (),
+    ("b0",),
+    (),
+    ("a1",),
+    (),
+    ("b1",),
+    (),
+    ("a0", "a1", "c1", "b0", "p0", "a0", "b1", "c0",),
+    ("a1", "c1",),
+    (),
+    ("b0",),
+    ("a0",),
+    ("p0", "b1", "a1",),
+    ("c1",),
+    ("a0",),
+    (),
+    ("c0", "p0",),
+    ("b0", "q0", "c1",),
+    ("a0", "b1", "c0",),
+    ("p0", "a1", "c1",),
+    ("t0", "b0",),
+    (
+        "p0", "c1", "q0", "s", "c0", "t1", "p0", "b0", "t0", "c1", "q0", "s", "c0", "t1", "q0",
+        "p0", "t0", "s", "c0", "t1", "c1", "t0", "q0",
+    ),
+)
 
 
 def dot(a, b, dims):
@@ -150,25 +195,28 @@
 
 class Chains:
     def __init__(self):
-        self.queue = []
-
-    def add(self, *chains):
-        for chain in chains:
-            next(chain)
-            self.queue.append(chain)
-
-    def tick(self, n=1):
-        for _ in range(min(n, len(self.queue))):
-            chain = self.queue.pop(0)
-            try:
-                next(chain)
-                self.queue.append(chain)
-            except StopIteration:
-                pass
+        self.running = {}
+        self.place = 0
+
+    def add(self, name, chain):
+        next(chain)
+        self.running[name] = chain
+
+    def advance(self, name):
+        if name in self.running and next(self.running[name], "ended") == "ended":
+            del self.running[name]
+
+    def tick(self):
+        for name in SCRIPT[self.place]:
+            self.advance(name)
+        self.place += 1
 
     def drain(self):
-        while self.queue:
-            self.tick()
+        assert self.place == len(SCRIPT) - 1
+        self.tick()
+        while self.running:
+            for name in tuple(self.running):
+                self.advance(name)
 
 
 def layer_kernel(
@@ -247,7 +295,7 @@
     cross_kept.wait()
     crossing = [wire.send(xcross.at[part], xrow.at[own, part], "zh") for part in (upper, lower)]
     own_kept.wait()
-    first = {"y": wire.send(xrow.at[own], xrow.at[own], "y")}
+    first = {name: wire.send(xrow.at[own], xrow.at[own], name) for name in PEERS}
     own_mate = wire.send(xrow.at[own], xrow.at[own], "core")
     early = [
         wire.send(wk_h, columns(wk), "core"),
@@ -302,8 +350,6 @@
 
     own_mate.wait_recv()
     project(seq)
-    for name in ("zl", "diag"):
-        first[name] = wire.send(xrow.at[own], xrow.at[own], name)
     first["y"].wait_recv()
     mates = {"y": to_mate(beyond(seq, "y"))}
     second = {name: [] for name in PEERS}
@@ -387,10 +433,11 @@
         part_sum[p] = summed
         return carry
 
-    lax.fori_loop(0, pairs, near_pair, 0)
+    lax.fori_loop(0, pairs // 2, near_pair, 0)
     for name in PEERS:
         arrive(second[name])
         mates[name] = to_mate(beyond(pseq, name))
+    lax.fori_loop(pairs // 2, pairs, near_pair, 0)
     for name in PEERS:
         mates[name].wait_recv()
         project(beyond(pseq, name))
@@ -466,7 +513,8 @@
         keep(wg_out.at[whole], wg_h.at[whole])
 
     def start_weights(wave):
-        chains.add(*[weights_chain(low, size, order) for low, size, order in wave])
+        for name, low, size, order in PARTS[wave]:
+            chains.add(name, weights_chain(low, size, order))
 
     finished = len(kept)
     mixed = (att[...] * live).astype(BF)
@@ -500,13 +548,17 @@
                 wg[m, pl.ds(2048 * r + b * 512, 512), :] = up_grad[:, at]
                 wg[m, pl.ds(2048 * r + 1024 + b * 512, 512), :] = down_grad[:, at]
             sv[6 + j : 7 + j, :] = column_sum(grad_inner.astype(F32))
-        start_weights((WAVE_ONE, WAVE_TWO)[r])
-        chains.tick(3 * r)
+            if r == 1 and m == 0:
+                chains.tick()
+        start_weights("ab"[r])
+        if r == 1:
+            chains.tick()
     out = unit_result.astype(BF)
     result2[0] = out[:BLOCK]
     result2[1] = out[BLOCK:]
     result_back = wire.send(result2.at[1], res_out.at[g], "zh")
     res_out[g] = out[:BLOCK]
+    chains.tick()
     cot_f = cotangent.astype(F32)
     grad_residual = cot_f + normalise_back(grad_normed2 * gain2, hat2, rstd2)
     sv[2:3, :] = column_sum(grad_normed2 * hat2)
@@ -518,7 +570,8 @@
     for m in range(2):
         for b in range(2):
             wg[m, pl.ds(OUT_AT + b * 256, 256), :] = out_grad[m * 256 : (m + 1) * 256, b * 256 : (b + 1) * 256]
-    start_weights(WAVE_THREE)
+    start_weights("c")
+    chains.tick()
     att[...] = dot(branch_grad, wo[...], NT).astype(BF).astype(F32) * live
 
     def back(p):
@@ -540,7 +593,7 @@
             dkv[p, chunk(c), 0:PAIR] = dot(grad_scores, query, NN).astype(BF)
             dkv[p, chunk(c), PAIR:] = dot(probs.astype(BF), grads, NN).astype(BF)
             query_grad = query_grad + dot(keys, grad_scores, TN)
-            chains.tick(2)
+            chains.tick()
         joined = join_heads_t(query_grad) * scale
         dq_ref[:, at] = jnp.transpose(joined).astype(BF)
 
@@ -555,7 +608,8 @@
             pair_grad = dot(normed_q, dq_ref[:, lanes_of(p)], TN).astype(BF)
             wg[m, pl.ds(PAIR_AT[n] + d, d // 2), 0:PAIR] = pair_grad[: d // 2]
             wg[m, pl.ds(PAIR_AT[n] + d, d // 2), PAIR:] = pair_grad[d // 2 :]
-        start_weights(WAVE_PAIR[n])
+        start_weights("pq"[n])
+        chains.tick()
 
     def tokens_back(grad_normed, block):
         hat, rstd = normalise(hidden_of(block))
@@ -575,9 +629,8 @@
     token_sum = column_sum(token_grad)
     value_sums = [jnp.zeros((1, PAIR), F32) for _ in range(pairs)]
 
-    def tokens_chain(hi, dims):
+    def tokens_chain(hi, one, leaves):
         slot = wire.slot()
-        one, two = dims
         copy = wire.send(t_out.at[hi, :, :, 1 - mp], t_core.at[hi], "core", slot)
         yield
         copy.wait_recv()
@@ -601,14 +654,14 @@
         yield
         copy.wait_recv()
         t_acc[hi, zl, y] += t_step[hi, 2]
-        if two == "zl":
+        if leaves:
             copy = wire.send(t_acc.at[hi, zl, y], tg_out.at[g], "zh", slot)
             yield
             copy.wait_recv()
         else:
             tg_out[g] = t_acc[hi, zl, y]
 
-    for hi, dims in ((1 - g, ("y", "zl")), (g, ("zl", "y"))):
+    for n, (hi, one) in enumerate(((1 - g, "zl"), (g, "y"))):
         for c in range(2):
             place = 2 * hi + c
             at = pl.ds(pl.multiple_of(place * step, step), step)
@@ -625,7 +678,7 @@
             for i in range(nb):
                 t_out[hi, c, i // 2, i % 2] = token_grad[i].astype(BF)
             chains.tick()
-        chains.add(tokens_chain(hi, dims))
+        chains.add(("t0", "t1")[n], tokens_chain(hi, one, n == 0))
     value_sum = jnp.concatenate(value_sums, axis=1)
 
     sv[0:1, :] = gain_sum
@@ -657,7 +710,7 @@
         sv_out[...] = sv_acc[len(stages)]
         result_back.wait_recv()
 
-    chains.add(vectors_chain())
+    chains.add("s", vectors_chain())
     chains.drain()
     wire.finish()
     for copy in kept[finished:]:

time: 129 us -> 120 us (0.930)
  Pallas kernels: 128 us -> 119 us
    pallas_call x1, Pallas kernels: 121 us -> 112 us  [layer(): pl.pallas_call(functools.partial(layer_kernel, has_x), out_shape=(shape((...]
where the time goes in v1:
time: 120 us
  Pallas kernels  119 us (99%)
    pallas_call x1, Pallas kernels, layer(): pl.pallas_call(functools.partial(layer_kernel, has_x), out_shape=(shape((...  112 us
    pallas_call x1, Pallas kernels, finish(): pl.pallas_call(functools.partial(finish_kernel, table_rows), out_shape=tu...  6.86 us

profile of v1, /device:TPU:0, one launch (start us, length us, event | category | flops | bytes accessed | tf_op | source)
XLA Modules:
  0.0 119.7 jit_solution(9293507159181940326)
XLA Ops:
  0.7 112.0 %layer.1 = (bf16[6144,256]{1,0:T(8,128)(2,1)}, f32[24,512]{1,0:T(8,128)}, bf16[2,128,512]{2,1,0:T(8,128)(2,1)}, bf16[2,128,512]{2,1,0:T(8,128)(2,1)}) custom-call(bf16[2,128,512]{2,1,0:T(8,128)(2,1)} %tokens.1, bf16[2,128,512]{2,1,0:T(8,128)(2,1)} %cot.1, bf16[512,256]{1,0:T(8,128)(2,1)} %wq_h.1, bf16[512,256]{1,0:T(8,128)(2,1)} %wk_h.1, ...), custom_call_target="tpu_custom_call" | custom-call | tf_op jit(solution)/shard_map/layer/pallas_call | solution.py:731
  112.6 6.9 %finish.1 = (bf16[2,128,512]{2,1,0:T(8,128)(2,1)}, f32[2,128,512]{2,1,0:T(8,128)}, f32[1000,512]{1,0:T(8,128)}, f32[512,256]{1,0:T(8,128)}, f32[512,256]{1,0:T(8...) custom-call(bf16[6144,256]{1,0:T(8,128)(2,1)} %get-tuple-element.40., ...), custom_call_target="tpu_custom_call" | custom-call | tf_op jit(solution)/shard_map/finish/pallas_call | solution.py:878

commit v2 on v1

--- a/solution.py
+++ b/solution.py
@@ -21,24 +21,24 @@
 GELU_C = math.sqrt(2.0 / math.pi)
 OUT_AT, PAIR_AT, PAIR_ROWS, WG_ROWS = 4096, (4608, 5376), 768, 6144
 SV_TABLE = 16
-RECEIVES, SENDS, KEEPS = 132, 48, 30
-SPANS_AT, ROWS_AT = 128, 144
+RECEIVES, SENDS, KEEPS = 146, 44, 22
+SPAN_ROWS = 16
 PEERS = ("y", "zl", "diag")
 PARTS = {
     "a": (
-        ("a0", 0, 768, (("zl",), ("x", "y",), ("zh",),)),
-        ("a1", 768, 768, (("x",), ("y",), ("zl", "zh",),)),
+        ("a0", 0, 768, (("x",), ("y",), ("zl", "zh",),)),
+        ("a1", 768, 768, (("zl",), ("x", "y",), ("zh",),)),
     ),
     "b": (
-        ("b0", 1536, 768, (("x",), ("y",), ("zl", "zh",),)),
-        ("b1", 2304, 768, (("x", "y",), ("zl", "zh",),)),
+        ("b0", 1536, 768, (("x",), ("zl",), ("y",), ("zh",),)),
+        ("b1", 2304, 768, (("zl",), ("x", "y",), ("zh",),)),
     ),
     "c": (
-        ("c0", 3072, 768, (("x",), ("zl", "zh",), ("y",),)),
-        ("c1", 3840, 768, (("y",), ("x",), ("zl",), ("zh",),)),
+        ("c0", 3072, 768, (("x", "y",), ("zl", "zh",),)),
+        ("c1", 3840, 768, (("x",), ("zl",), ("y",), ("zh",),)),
     ),
     "p": (
-        ("p0", 4608, 768, (("x",), ("y",), ("zl", "zh",),)),
+        ("p0", 4608, 768, (("y",), ("x",), ("zl", "zh",),)),
     ),
     "q": (
         ("q0", 5376, 768, (("x", "y",), ("zl", "zh",),)),
@@ -50,30 +50,30 @@
     (),
     (),
     ("a0", "a1", "c0", "c1",),
+    ("a0", "b1", "b0", "a1",),
     (),
-    ("b0",),
     (),
-    ("a1",),
+    ("a0",),
+    ("b0", "a1", "c0",),
     (),
+    ("a0", "b0",),
+    ("a1", "c1",),
+    ("p0", "a0", "b1", "c0", "b0",),
+    ("a1", "c1",),
     ("b1",),
     (),
-    ("a0", "a1", "c1", "b0", "p0", "a0", "b1", "c0",),
-    ("a1", "c1",),
     (),
-    ("b0",),
-    ("a0",),
-    ("p0", "b1", "a1",),
+    ("c0", "p0", "a0", "b0",),
     ("c1",),
-    ("a0",),
     (),
-    ("c0", "p0",),
-    ("b0", "q0", "c1",),
-    ("a0", "b1", "c0",),
-    ("p0", "a1", "c1",),
-    ("t0", "b0",),
+    ("a1", "b1",),
+    ("q0", "c0", "c1", "b0",),
+    ("p0",),
+    ("c1",),
+    ("b1", "t0", "b0",),
     (
-        "p0", "c1", "q0", "s", "c0", "t1", "p0", "b0", "t0", "c1", "q0", "s", "c0", "t1", "q0",
-        "p0", "t0", "s", "c0", "t1", "c1", "t0", "q0",
+        "p0", "q0", "s", "c1", "t1", "b1", "b0", "p0", "t0", "q0", "s", "c1", "p0", "t0", "q0",
+        "t1", "c1", "s", "p0", "t0", "t1", "q0",
     ),
 )
 
@@ -224,7 +224,7 @@
     tokens, cot, wq_h, wk_h, wv_h, wo_h, up_h, down_h, table_h,
     segments, timesteps, gain_1, shift_1, gain_2, shift_2, out_bias_1, down_bias_1, query_bias_1, value_bias_1, up_bias_1,
     wg_h, sv_out, tg_out, res_out,
-    xrow, xcross, table, cot2, wq, wk, wv, wo, up, down, bias,
+    xrow, span, xcross, span_cross, table, cot2, wq, wk, wv, wo, up, down, bias,
     normed, normed_t, k_ref, v_ref, hot, s_buf, att, att_t, lse, q_ref, dkv, dq_ref, t_buf, part_top, part_sum,
     wg, acc, core_buf, step_buf, wg_out, t_out, t_core, t_acc, t_step, result2, sv_buf, sv_acc,
     send_sem, recv_sem, local_sem,
@@ -265,20 +265,14 @@
         for copy in copies:
             copy.wait_recv()
 
-    chars = pl.ds(0, BLOCK)
-    cross_kept = keep(tokens.at[1 - g], xcross.at[chars])
-    own_kept = keep(tokens.at[g], xrow.at[own, chars])
+    cross_kept = keep(tokens.at[1 - g], xcross)
+    own_kept = keep(tokens.at[g], xrow.at[own])
     early_kept = [keep(table_h, table), keep(wk_h, columns(wk)), keep(wv_h, columns(wv)), keep(wq_h, columns(wq))]
     spans = segments[...].astype(F32)
     first_row = jnp.where(g == 0, spans[0:1, :], spans[1:2, :])
     second_row = jnp.where(g == 0, spans[1:2, :], spans[0:1, :])
-    blank = jnp.zeros((ROWS_AT - SPANS_AT, d - BLOCK), F32)
-
-    def span_rows(row):
-        return jnp.concatenate([jnp.broadcast_to(row, (ROWS_AT - SPANS_AT, BLOCK)), blank], axis=1).astype(BF)
-
-    xcross[SPANS_AT:, :] = span_rows(second_row)
-    xrow[own, SPANS_AT:, :] = span_rows(first_row)
+    span_cross[...] = jnp.broadcast_to(second_row, (SPAN_ROWS, BLOCK)).astype(BF)
+    span[own] = jnp.broadcast_to(first_row, (SPAN_ROWS, BLOCK)).astype(BF)
 
     def line(ref):
         return ref[...].astype(F32).reshape(1, ref.shape[0])
@@ -291,12 +285,19 @@
     )
     greet(("core", "y", "zl", "diag", "zh", ("zl", "zh")) + (("x", ("x", "y")) if has_x else ()))
 
-    upper, lower = pl.ds(0, BLOCK // 2), pl.ds(BLOCK // 2, ROWS_AT - BLOCK // 2)
+    def pass_on(block, name):
+        return [
+            wire.send(span.at[block], span.at[block], name),
+            wire.send(xrow.at[block], xrow.at[block], name),
+        ]
+
+    halves = pl.ds(0, BLOCK // 2), pl.ds(BLOCK // 2, BLOCK // 2)
+    crossing_span = wire.send(span_cross, span.at[own], "zh")
     cross_kept.wait()
-    crossing = [wire.send(xcross.at[part], xrow.at[own, part], "zh") for part in (upper, lower)]
+    crossing = [wire.send(xcross.at[part], xrow.at[own, part], "zh") for part in halves]
     own_kept.wait()
-    first = {name: wire.send(xrow.at[own], xrow.at[own], name) for name in PEERS}
-    own_mate = wire.send(xrow.at[own], xrow.at[own], "core")
+    first = {name: pass_on(own, name) for name in PEERS}
+    own_mate = pass_on(own, "core")
     early = [
         wire.send(wk_h, columns(wk), "core"),
         wire.send(wv_h, columns(wv), "core"),
@@ -322,7 +323,7 @@
         return block.astype(F32) + row_embed
 
     def seg_column(b):
-        return jnp.transpose(xrow[b, SPANS_AT:, 0:BLOCK].astype(F32))[:, 0:1]
+        return jnp.transpose(span[b].astype(F32))[:, 0:1]
 
     arrive(early)
     query_bias = jnp.concatenate([bias[0, 0:1, :256], bias[1, 0:1, :256]], axis=1)
@@ -331,7 +332,7 @@
     def project(s):
         n = 2 * BLOCK
         at = pl.ds(pl.multiple_of(s * n, n), n)
-        hat, _ = normalise(hidden_of(xrow[pl.ds(2 * s, 2), 0:BLOCK, :].reshape(n, d)))
+        hat, _ = normalise(hidden_of(xrow[pl.ds(2 * s, 2)].reshape(n, d)))
         low = (hat * gain + shift).astype(BF)
         normed[at, :] = low
         normed_t[:, at] = jnp.transpose(low)
@@ -345,30 +346,30 @@
         return {"y": flip(base, 1), "zl": flip(base, 2), "diag": flip(flip(base, 1), 2)}[name]
 
     def to_mate(s):
-        block = xrow.at[2 * s + mp]
-        return wire.send(block, block, "core")
-
-    own_mate.wait_recv()
+        return pass_on(2 * s + mp, "core")
+
+    arrive(own_mate)
     project(seq)
-    first["y"].wait_recv()
+    arrive(first["y"])
     mates = {"y": to_mate(beyond(seq, "y"))}
-    second = {name: [] for name in PEERS}
-    for copy, part in zip(crossing, (upper, lower)):
+    crossing_span.wait_recv()
+    second = {name: [wire.send(span.at[par], span.at[par], name)] for name in PEERS}
+    for copy, part in zip(crossing, halves):
         copy.wait_recv()
         for name in PEERS:
             second[name].append(wire.send(xrow.at[par, part], xrow.at[par, part], name))
     par_mate = to_mate(pseq)
-    mates["y"].wait_recv()
+    arrive(mates["y"])
     project(beyond(seq, "y"))
     for name in ("zl", "diag"):
-        first[name].wait_recv()
+        arrive(first[name])
         mates[name] = to_mate(beyond(seq, name))
     late = [
         wire.send(src, dst, "core")
         for src, dst in ((wo_h, rows(wo)), (up_h, columns(up)), (down_h, rows(down)))
     ]
     late.append(wire.send(cot.at[1 - g], cot2.at[1], "zh"))
-    par_mate.wait_recv()
+    arrive(par_mate)
     project(pseq)
 
     def query_rows(ref):
@@ -380,7 +381,7 @@
     query_low = (dot(query_rows(normed), wq[...], NN) + query_bias).astype(BF)
     q_ref[...] = (query_low.astype(F32) * scale).astype(BF)
     for name in ("zl", "diag"):
-        mates[name].wait_recv()
+        arrive(mates[name])
         project(beyond(seq, name))
 
     spans_q = jnp.concatenate([seg_column(own), seg_column(par)], axis=0)
@@ -439,7 +440,7 @@
         mates[name] = to_mate(beyond(pseq, name))
     lax.fori_loop(pairs // 2, pairs, near_pair, 0)
     for name in PEERS:
-        mates[name].wait_recv()
+        arrive(mates[name])
         project(beyond(pseq, name))
     far = [beyond(pseq, name) for name in PEERS]
     def far_pair(p, carry):
@@ -518,7 +519,7 @@
 
     finished = len(kept)
     mixed = (att[...] * live).astype(BF)
-    hidden_q = hidden_of(jnp.concatenate([xrow[own, 0:BLOCK, :], xrow[par, 0:BLOCK, :]], axis=0))
+    hidden_q = hidden_of(jnp.concatenate([xrow[own], xrow[par]], axis=0))
     residual = hidden_q + dot(mixed, wo[...], NN) + line(out_bias_1)
     gain2, shift2 = line(gain_2), line(shift_2)
     hat2, rstd2 = normalise(residual)
@@ -528,10 +529,11 @@
     grad_normed2 = jnp.zeros((nq, d), F32)
     sv = sv_acc.at[0]
     for r in range(half // step):
-        for m in range(2):
-            j = (m * half + r * step) // step
-            units = pl.ds(j * step, step)
-            inner = dot(normed2, up[:, units], NN) + bias[m, 1 + r : 2 + r, :]
+        for k in range(2):
+            m = mp if k else 1 - mp
+            j = m * (half // step) + r
+            units = pl.ds(pl.multiple_of(j * step, step), step)
+            inner = dot(normed2, up[:, units], NN) + bias[m, pl.ds(1 + r, 1), :]
             square = inner * inner
             bent = jnp.tanh(GELU_C * inner * (1.0 + GELU_A * square))
             activated = (0.5 * inner * (1.0 + bent)).astype(BF)
@@ -547,12 +549,11 @@
                 at = slice(b * 256, (b + 1) * 256)
                 wg[m, pl.ds(2048 * r + b * 512, 512), :] = up_grad[:, at]
                 wg[m, pl.ds(2048 * r + 1024 + b * 512, 512), :] = down_grad[:, at]
-            sv[6 + j : 7 + j, :] = column_sum(grad_inner.astype(F32))
-            if r == 1 and m == 0:
+            sv_acc[0, pl.ds(6 + j, 1), :] = column_sum(grad_inner.astype(F32))
+            if r == 1:
                 chains.tick()
-        start_weights("ab"[r])
-        if r == 1:
-            chains.tick()
+            if k == 0:
+                start_weights("ab"[r])
     out = unit_result.astype(BF)
     result2[0] = out[:BLOCK]
     result2[1] = out[BLOCK:]
@@ -621,7 +622,7 @@
 
     query_grad = dq_ref[...]
     token_grad, gain_sum, shift_sum = tokens_back(
-        dot(query_grad, wq[...], NT), jnp.concatenate([xrow[own, 0:BLOCK, :], xrow[par, 0:BLOCK, :]], axis=0)
+        dot(query_grad, wq[...], NT), jnp.concatenate([xrow[own], xrow[par]], axis=0)
     )
     token_grad = token_grad + grad_residual
     t_buf[own] = token_grad[:BLOCK]
@@ -661,7 +662,7 @@
         else:
             tg_out[g] = t_acc[hi, zl, y]
 
-    for n, (hi, one) in enumerate(((1 - g, "zl"), (g, "y"))):
+    for n, (hi, one) in enumerate(((1 - g, "y"), (g, "y"))):
         for c in range(2):
             place = 2 * hi + c
             at = pl.ds(pl.multiple_of(place * step, step), step)
@@ -672,7 +673,7 @@
                 grad_normed = grad_normed + dot(pair_grad, both, NT)
                 value_sums[p] = value_sums[p] + column_sum(pair_grad[:, PAIR:].astype(F32))
             blocks_at = pl.ds(place * nb, nb)
-            token_grad, a, b = tokens_back(grad_normed, xrow[blocks_at, 0:BLOCK, :].reshape(step, d))
+            token_grad, a, b = tokens_back(grad_normed, xrow[blocks_at].reshape(step, d))
             gain_sum, shift_sum, token_sum = gain_sum + a, shift_sum + b, token_sum + column_sum(token_grad)
             token_grad = t_buf[blocks_at] + token_grad.reshape(nb, BLOCK, d)
             for i in range(nb):
@@ -739,8 +740,10 @@
         in_specs=any_spec(len(big)) + vmem_spec(len(small)),
         out_specs=tuple(any_spec(1) + vmem_spec(3)),
         scratch_shapes=[
-            vmem((blocks, ROWS_AT, d), BF),
-            vmem((ROWS_AT, d), BF),
+            vmem((blocks, BLOCK, d), BF),
+            vmem((blocks, SPAN_ROWS, BLOCK), BF),
+            vmem(block, BF),
+            vmem((SPAN_ROWS, BLOCK), BF),
             vmem(table.shape, BF),
             vmem((2,) + block, BF),
             vmem((d, d), BF),
@@ -815,7 +818,12 @@
     ids = sv[12:13, 0:128]
     spread = jnp.where(lax.broadcasted_iota(jnp.int32, (table_v.shape[0], 128), 0).astype(F32) == ids, 1.0, 0.0)
     sums = jnp.concatenate([sv[SV_TABLE:, :], jnp.zeros((128 - (sv.shape[0] - SV_TABLE), sv.shape[1]), F32)], axis=0)
-    table_v[...] = lax.dot_general(spread, sums, NN, precision=lax.Precision.HIGHEST, preferred_element_type=F32)
+    spread = spread.astype(BF)
+    high = sums.astype(BF)
+    rest = sums - high.astype(F32)
+    middle = rest.astype(BF)
+    low = (rest - middle.astype(F32)).astype(BF)
+    table_v[...] = dot(spread, high, NN) + (dot(spread, middle, NN) + dot(spread, low, NN))
     leave(table_v, table_o)
 
     def flat(ref, value):

time: 120 us -> 116 us (0.967)
  Pallas kernels: 119 us -> 115 us
    pallas_call x1, Pallas kernels: 112 us -> 109 us  [layer(): pl.pallas_call(functools.partial(layer_kernel, has_x), out_shape=(shape((...]
where the time goes in v2:
time: 116 us
  Pallas kernels  115 us (99%)
    pallas_call x1, Pallas kernels, layer(): pl.pallas_call(functools.partial(layer_kernel, has_x), out_shape=(shape((...  109 us
    pallas_call x1, Pallas kernels, finish(): pl.pallas_call(functools.partial(finish_kernel, table_rows), out_shape=tu...  6.08 us

profile of v2, /device:TPU:0, one launch (start us, length us, event | category | flops | bytes accessed | tf_op | source)
XLA Modules:
  0.0 115.8 jit_solution(16572569678311607254)
XLA Ops:
  0.7 108.9 %layer.1 = (bf16[6144,256]{1,0:T(8,128)(2,1)}, f32[24,512]{1,0:T(8,128)}, bf16[2,128,512]{2,1,0:T(8,128)(2,1)}, bf16[2,128,512]{2,1,0:T(8,128)(2,1)}) custom-call(bf16[2,128,512]{2,1,0:T(8,128)(2,1)} %tokens.1, bf16[2,128,512]{2,1,0:T(8,128)(2,1)} %cot.1, bf16[512,256]{1,0:T(8,128)(2,1)} %wq_h.1, bf16[512,256]{1,0:T(8,128)(2,1)} %wk_h.1, ...), custom_call_target="tpu_custom_call" | custom-call | tf_op jit(solution)/shard_map/layer/pallas_call | solution.py:732
  109.5 6.1 %finish.1 = (bf16[2,128,512]{2,1,0:T(8,128)(2,1)}, f32[2,128,512]{2,1,0:T(8,128)}, f32[1000,512]{1,0:T(8,128)}, f32[512,256]{1,0:T(8,128)}, f32[512,256]{1,0:T(8...) custom-call(bf16[6144,256]{1,0:T(8,128)(2,1)} %get-tuple-element.40., ...), custom_call_target="tpu_custom_call" | custom-call | tf_op jit(solution)/shard_map/finish/pallas_call | solution.py:886

commit v3 on v2

--- a/solution.py
+++ b/solution.py
@@ -434,11 +434,10 @@
         part_sum[p] = summed
         return carry
 
-    lax.fori_loop(0, pairs // 2, near_pair, 0)
-    for name in PEERS:
+    for n, name in enumerate(PEERS):
+        lax.fori_loop((0, 2, 3)[n], (2, 3, pairs)[n], near_pair, 0)
         arrive(second[name])
         mates[name] = to_mate(beyond(pseq, name))
-    lax.fori_loop(pairs // 2, pairs, near_pair, 0)
     for name in PEERS:
         arrive(mates[name])
         project(beyond(pseq, name))
@@ -813,8 +812,8 @@
         copy.start()
         leaving.append(copy)
 
+    coming_tg, coming_res = fetch(tg, tg_v, parts), fetch(res, res_v, parts + 1)
     coming = [fetch(wg.at[pl.ds(i * rows, rows)], wg_v.at[pl.ds(i * rows, rows)], i) for i in range(parts)]
-    coming_tg, coming_res = fetch(tg, tg_v, parts), fetch(res, res_v, parts + 1)
     ids = sv[12:13, 0:128]
     spread = jnp.where(lax.broadcasted_iota(jnp.int32, (table_v.shape[0], 128), 0).astype(F32) == ids, 1.0, 0.0)
     sums = jnp.concatenate([sv[SV_TABLE:, :], jnp.zeros((128 - (sv.shape[0] - SV_TABLE), sv.shape[1]), F32)], axis=0)
@@ -838,6 +837,11 @@
     def take(at, n):
         return wg_v[at : at + n, :].astype(F32)
 
+    coming_res.wait()
+    leave(res_v, res_o)
+    coming_tg.wait()
+    tg_f[...] = tg_v[...].astype(F32)
+    leave(tg_f, tg_o)
     for i in range(parts):
         coming[i].wait()
         if i in (0, 2):
@@ -864,11 +868,6 @@
             leave(wk_v, wk_o)
             leave(wv_v, wv_o)
             leave(wq_v, wq_o)
-    coming_res.wait()
-    leave(res_v, res_o)
-    coming_tg.wait()
-    tg_f[...] = tg_v[...].astype(F32)
-    leave(tg_f, tg_o)
     for copy in leaving:
         copy.wait()
 

time: 116 us -> 115 us (level)
  no operation moved by 1% of the time
where the time goes in v3:
time: 115 us
  Pallas kernels  114 us (99%)
    pallas_call x1, Pallas kernels, layer(): pl.pallas_call(functools.partial(layer_kernel, has_x), out_shape=(shape((...  108 us
    pallas_call x1, Pallas kernels, finish(): pl.pallas_call(functools.partial(finish_kernel, table_rows), out_shape=tu...  6.07 us

profile of v3, /device:TPU:0, one launch (start us, length us, event | category | flops | bytes accessed | tf_op | source)
XLA Modules:
  0.0 114.8 jit_solution(8197953662362667235)
XLA Ops:
  0.7 107.9 %layer.1 = (bf16[6144,256]{1,0:T(8,128)(2,1)}, f32[24,512]{1,0:T(8,128)}, bf16[2,128,512]{2,1,0:T(8,128)(2,1)}, bf16[2,128,512]{2,1,0:T(8,128)(2,1)}) custom-call(bf16[2,128,512]{2,1,0:T(8,128)(2,1)} %tokens.1, bf16[2,128,512]{2,1,0:T(8,128)(2,1)} %cot.1, bf16[512,256]{1,0:T(8,128)(2,1)} %wq_h.1, bf16[512,256]{1,0:T(8,128)(2,1)} %wk_h.1, ...), custom_call_target="tpu_custom_call" | custom-call | tf_op jit(solution)/shard_map/layer/pallas_call | solution.py:731
  108.6 6.1 %finish.1 = (bf16[2,128,512]{2,1,0:T(8,128)(2,1)}, f32[2,128,512]{2,1,0:T(8,128)}, f32[1000,512]{1,0:T(8,128)}, f32[512,256]{1,0:T(8,128)}, f32[512,256]{1,0:T(8...) custom-call(bf16[6144,256]{1,0:T(8,128)(2,1)} %get-tuple-element.40., ...), custom_call_target="tpu_custom_call" | custom-call | tf_op jit(solution)/shard_map/finish/pallas_call | solution.py:885
